TPU v7x, 256 devices: a whole 4x4x8 slice. The times are simulated.
256 devices in a mesh: dp: 32 (over z, y), tensor: 8 (over x, core).
Axes of the slice: x: 4, y: 4, z: 8, core: 2. Of those that a mesh axis runs over, the one named last changes fastest.
Arguments:
- activations: bfloat16 [8192, 4096], P('dp'), may hold values from -6 to 6
- cotangent: bfloat16 [8192, 7168], P('dp', 'tensor'), may hold values from -0.625 to 0.625
- old_gate_up: bfloat16 [4096, 2, 28672], P('dp', None, 'tensor'), may hold values from -0.09375 to 0.09375
- kept_index: int32 [7168], replicated, may hold values from 0 to 28671, as said below
- new_slot: int32 [7168], replicated, may hold values from 0 to 7167, as said below
Outputs:
- student_gate_up: bfloat16 [4096, 2, 7168], P('dp', None, 'tensor')
- hidden: bfloat16 [8192, 7168], P('dp', 'tensor')
- weight_grad: bfloat16 [4096, 2, 7168], P('dp', None, 'tensor')
Inputs may be any that keep to these rules, and one draw needn't show every extreme that they name: `kept_index`: distinct and ascending. Old owner of teacher neuron i is i // 3584. `new_slot`: A permutation; new owner of student position j is j // 896. No old owner sends more than 168 kept neurons to one new owner, and every new owner receives exactly 168 from some old owner.
All inputs are finite; a program needn't handle non-finite values.
Results may differ from a plain program's by a relative error of at most 0.024.
Values may be sent and summed in bfloat16 or wider, within the bound.
A program may use at most 128 MiB of HBM per device.

v0:
```python
import jax
import jax.numpy as jnp
from jax import lax
from jax.sharding import PartitionSpec as P


def per_device(activations, cotangent, old_gate_up, kept_index, new_slot):
    tensor_size = lax.axis_size("tensor")
    tensor_rank = lax.axis_index("tensor")
    own_columns = old_gate_up.shape[0]
    own_rows = old_gate_up.shape[2]
    keep_total = kept_index.shape[0]
    own_width = keep_total // tensor_size
    base_count = keep_total // (tensor_size * tensor_size)
    capacity = base_count + base_count // 2
    old_owner = kept_index // own_rows
    new_owner = new_slot // own_width
    pair_index = old_owner * tensor_size + new_owner
    pair_table = (
        pair_index[:, None] == jnp.arange(tensor_size * tensor_size, dtype=jnp.int32)[None, :]
    ).astype(jnp.int32)
    slot_rank = jnp.sum(jnp.cumsum(pair_table, axis=0) * pair_table, axis=1) - 1
    is_mine = old_owner == tensor_rank
    target_place = jnp.where(is_mine, new_owner * capacity + slot_rank, tensor_size * capacity)
    local_row = jnp.where(is_mine, kept_index - tensor_rank * own_rows, 0)
    source_row = (
        jnp.zeros((tensor_size * capacity,), jnp.int32).at[target_place].set(local_row, mode="drop")
    )
    filled = (
        jnp.zeros((tensor_size * capacity,), jnp.bfloat16)
        .at[target_place]
        .set(jnp.ones((keep_total,), jnp.bfloat16), mode="drop")
    )
    outgoing = jnp.take(old_gate_up, source_row, axis=2) * filled
    received = lax.all_to_all(outgoing, "tensor", split_axis=2, concat_axis=2, tiled=True)
    inverse_order = (
        jnp.zeros((keep_total,), jnp.int32)
        .at[new_slot]
        .set(jnp.arange(keep_total, dtype=jnp.int32))
    )
    my_kept = lax.dynamic_slice_in_dim(inverse_order, tensor_rank * own_width, own_width)
    take_place = old_owner[my_kept] * capacity + slot_rank[my_kept]
    student_gate_up = jnp.take(received, take_place, axis=2)
    shard_piece = lax.all_gather(student_gate_up, "dp", axis=0, tiled=True)
    x_cols = activations
    gate_up = jnp.dot(
        x_cols,
        shard_piece.reshape(shard_piece.shape[0], 2 * own_width),
        preferred_element_type=jnp.float32,
    )
    gate_value = gate_up[:, :own_width]
    up_value = gate_up[:, own_width:]
    sigmoid = jax.nn.sigmoid(gate_value)
    silu_value = gate_value * sigmoid
    hidden = (silu_value * up_value).astype(jnp.bfloat16)
    incoming = cotangent.astype(jnp.float32)
    grad_gate = incoming * up_value * sigmoid * (1.0 + gate_value * (1.0 - sigmoid))
    grad_up = incoming * silu_value
    pre_grads = jnp.concatenate([grad_gate, grad_up], axis=1).astype(jnp.bfloat16)
    x_cols = activations
    summed = lax.psum_scatter(
        lax.dot_general(
            x_cols, pre_grads, (((0,), (0,)), ((), ())), preferred_element_type=jnp.float32
        ).astype(jnp.bfloat16),
        "dp",
        scatter_dimension=0,
        tiled=True,
    )
    weight_grad = summed.reshape(own_columns, 2, own_width)
    return (student_gate_up, hidden, weight_grad)


def solution(mesh):
    placed = (P("dp", None), P("dp", "tensor"), P("dp", None, "tensor"), P(), P())
    return jax.shard_map(
        per_device,
        mesh=mesh,
        in_specs=placed,
        out_specs=(P("dp", None, "tensor"), P("dp", "tensor"), P("dp", None, "tensor")),
        check_vma=False,
    )
```

profile of v0, /device:TPU:32, one launch (start us, length us, event | category | flops | bytes accessed | tf_op | source)
XLA Modules:
  0.0 847.5 jit_solution(14123652462253376690)
XLA Ops:
  7.2 0.0 copy-start
  7.2 0.9 subtract_select_fusion
  8.1 0.8 multiply_add_fusion
  8.9 1.3 fusion.3
  10.2 36.1 %reduce-window.6 = s32[64,56,128]{2,1,0:T(8,128)} reduce-window(s32[64,56,128]{2,1,0:T(8,128)} %fusion.3, s32[]{:T(128)} %constant.30.clone.1), window={size=1x1x128 pad=0_0x0_0x127_0}, to_apply=%region_1.2 | reduce-window | flops 58261504 | bytes 3670020 | tf_op jit(solution)/shard_map/reduce-window
  46.4 3.3 slice.24
  49.6 2.1 copy.34
  51.7 0.2 reduce-window.9
  52.0 1.8 broadcast_add_fusion
  53.8 0.0 copy-start.2
  53.8 0.4 fusion.2
  54.2 0.3 copy-done.2
  54.6 26.7 %scatter_custom_fusion.1 = s32[1344]{0:T(1024)S(1)} fusion(s32[7168]{0:T(1024)S(1)} %get-tuple-element.24, s32[7168]{0:T(1024)S(1)} %get-tuple-element.17, s32[]{:T(128)} %constant.30.clone.1), kind=kCustom, calls=%fused_computation.57 | custom fusion | bytes 5380 | tf_op jit(solution)/shard_map/scatter | solution.py:27
  81.4 7.3 copy.28
  88.7 49.5 %scatter_custom_fusion.2 = bf16[1344]{0:T(1024)(128)(2,1)S(1)} fusion(s32[7168]{0:T(1024)S(1)} %get-tuple-element.24, bf16[7168]{0:T(1024)(128)(2,1)S(1)} %broadcast.79, bf16[]{:T(256)} %constant.73.clone.1), kind=kCustom, calls=%fused_computation.62 | custom fusion | bytes 2690 | tf_op jit(solution)/shard_map/scatter | solution.py:32
  138.2 4.2 gather_fusion.2
  142.4 8.4 multiply_bitcast_fusion
  150.8 4.3 all-to-all-start
  155.1 0.0 all-gather.2.cloned.1.call-start
  155.2 26.9 %scatter_custom_fusion = s32[7168]{0:T(1024)S(1)} fusion(s32[7168]{0:T(1024)S(1)} %get-tuple-element.23, s32[7168]{0:T(1024)S(1)} %iota.11, s32[]{:T(128)} %constant.30.clone.1), kind=kCustom, calls=%fused_computation.49 | custom fusion | bytes 28676 | tf_op jit(solution)/shard_map/scatter | solution.py:39
  182.1 0.1 compare_select_fusion.5
  182.2 5.2 gather_fusion
  187.4 5.2 gather_fusion.1
  192.6 0.0 all-to-all-done
  192.6 3.6 gather_fusion.3
  196.2 3.9 fusion.12
  200.1 0.0 all-gather.2.cloned.1.call-update
  200.1 0.0 reduce-scatter.4.cloned.1.call-start
  200.2 1.2 copy.30
  201.4 351.1 %all-gather.2.cloned.1.call-done = bf16[4096,2,896]{0,1,2:T(2,128)(2,1)} async-done(((bf16[128,2,896]{0,1,2:T(2,128)(2,1)}), bf16[4096,2,896]{0,1,2:T(2,128)(2,1)}) %all-gather.2.cloned.1.call-update) | async-done | bytes 14680080 | tf_op jit(solution)/shard_map/all_gather | solution.py:44
  552.5 13.1 %copy.29 = bf16[4096,2,896]{0,2,1:T(8,128)(2,1)S(1)} copy(bf16[4096,2,896]{0,1,2:T(2,128)(2,1)} %all-gather.2.cloned.1.call-done) | data formatting | bytes 29360128 | tf_op jit(solution)/shard_map/all_gather | solution.py:44
  565.6 0.0 copy-done
  565.6 4.3 convolution_bitcast_fusion
  569.9 0.7 fusion.6
  570.6 8.3 fusion
  578.9 18.8 %copy.35 = bf16[4096,1792]{1,0:T(8,128)(2,1)} copy(bf16[4096,1792]{0,1:T(8,128)(2,1)} %fusion) | data formatting | bytes 29360128
  597.6 0.0 copy-start.1
  597.6 0.0 reduce-scatter.4.cloned.1.call-update
  597.6 1.0 copy-done.1
  598.6 2.2 copy.31
  600.8 1.0 copy.32
  601.8 236.3 %reduce-scatter.4.cloned.1.call-done = bf16[128,1792]{1,0:T(8,128)(2,1)} async-done(((bf16[4096,1792]{1,0:T(8,128)(2,1)}), bf16[128,1792]{1,0:T(8,128)(2,1)}) %reduce-scatter.4.cloned.1.call-update) | async-done | bytes 458768
  838.1 1.3 copy.36
  839.4 1.2 copy.33
  (10 shorter events, 0.1 us)
Async XLA Ops:
  7.2 558.4 %copy-start = (bf16[256,4096]{1,0:T(8,128)(2,1)S(1)}, bf16[256,4096]{1,0:T(8,128)(2,1)}, u32[]{:S(2)}) copy-start(bf16[256,4096]{1,0:T(8,128)(2,1)} %param.5) | copy-start | bytes 6291460
  53.8 0.8 copy-start.2
  150.8 41.8 %all-to-all-start = ((bf16[128,2,1344]{0,1,2:T(2,128)(2,1)}), bf16[128,2,1344]{0,1,2:T(2,128)(2,1)S(1)}, u32[]{:S(2)}, u32[]{:S(2)}) async-start(bf16[128,2,1344]{0,1,2:T(2,128)(2,1)} %multiply_bitcast_fusion), calls=%async_computation | async-start | bytes 1376256 | tf_op jit(solution)/shard_map/all_to_all | solution.py:35
  155.1 397.4 %all-gather.2.cloned.1.call-start = ((), (), s32[]{:S(2)}) async-start(), calls=%async_computation.2 | async-start | bytes 15138816 | tf_op jit(solution)/shard_map/all_gather | solution.py:44
  200.1 638.0 %reduce-scatter.4.cloned.1.call-start = ((), (), s32[]{:S(2)}) async-start(), calls=%async_computation.3 | async-start | bytes 15138816
  597.6 1.0 copy-start.1
Sparse Core Ops, SparseCore 0:
  200.3 352.2 all-gather.1
  597.8 240.3 reduce-scatter.3
where the time goes:
time: 854 us; the launch traced here: 848 us
  waiting for transfers between devices  588 us (69%)
  local copies, waits for them, and re-layouts  174 us (20%)
  other arithmetic  54.8 us (6%)
  between operations  14.2 us (2%)
  matrix products  12.6 us (1%)
    all_gather x1, waiting for transfers between devices, per_device(): shard_piece = lax.all_gather(student_gate_up, 'dp', axis=0, tiled=True)  351 us
    unnamed x3, waiting for transfers between devices  236 us
    scatter x1, local copies, waits for them, and re-layouts, per_device(): filled = jnp.zeros((tensor_size * capacity,), jnp.bfloat16).at[target_pla...  49.5 us
    another operation x4, other arithmetic  38.8 us
    unnamed x13, local copies, waits for them, and re-layouts  34.3 us
    scatter x1, local copies, waits for them, and re-layouts, per_device(): inverse_order = jnp.zeros((keep_total,), jnp.int32).at[new_slot].set(jnp....  26.9 us
    scatter x1, local copies, waits for them, and re-layouts, per_device(): jnp.zeros((tensor_size * capacity,), jnp.int32).at[target_place]  26.7 us
  transfers between devices with their start and end apart: 3, of which 2 were waited for; matrix products, arithmetic and copies ran while one was open for 5% of the time, Pallas kernels for 0%

commit v1 on v0

v1 whole, which is shorter than its diff:
```python
import jax
import jax.numpy as jnp
from jax import lax
from jax.experimental import pallas as pl
from jax.experimental.pallas import tpu as pltpu
from jax.sharding import PartitionSpec as P

MESH = pl.DeviceIdType.MESH
NZ, NY, NX, NC = 8, 4, 4, 2
NT = NX * NC
D = 4096
KEEP = 7168
OWN = 896
ROWS = 3584
CAP = 176
PLACES = NT * CAP
EIGHTH = OWN // NZ
BLK = 128
TOK = NZ * BLK
CHUNK = D // NY
KB = KEEP // 128
F32 = jnp.float32
BF = jnp.bfloat16


def iota(shape, dim):
    return lax.broadcasted_iota(jnp.int32, shape, dim)


def dot(a, b):
    return lax.dot_general(a, b, (((1,), (0,)), ((), ())), preferred_element_type=F32)


def dot_nt(a, b):
    return lax.dot_general(a, b, (((1,), (1,)), ((), ())), preferred_element_type=F32)


def onehot(cond):
    return jnp.where(cond, 1.0, 0.0).astype(BF)


def interleave_matrix():
    a = iota((256, 256), 0)
    return onehot(iota((256, 256), 1) == (a & 1) * 128 + (a >> 1))


def mm(i, m=128):
    return pl.multiple_of(i, m)


class Sems:
    def __init__(self, ref):
        self.ref, self.n = ref, 0

    def take(self, count=1):
        first = self.n
        self.n += count
        return first


def kernel(act, cot, old, kept, slot, stu, hid, wg,
           a_in, c_in, o_in, krow, srow, ab, idx, ohs, inc, pb, rts, rr, stn, st2, wt, ct, cb,
           hs, hr, dg, cs, cx, pa, rb_send, rb, rc_send, rc, fg, gr,
           load_sems, send_sems, recv_sems):
    dp = lax.axis_index("dp")
    t = lax.axis_index("tensor")
    z, y = dp // NY, dp % NY
    x, c = t // NC, t % NC

    def dev(x_, c_, y_, z_):
        return (z_ * NY + y_, x_ * NC + c_)

    sib = dev(x, 1 - c, y, z)
    z_up, z_dn = dev(x, c, y, (z + 1) % NZ), dev(x, c, y, (z + NZ - 1) % NZ)
    y_up, y_dn = dev(x, c, (y + 1) % NY, z), dev(x, c, (y + NY - 1) % NY, z)

    ssem, rsem = Sems(send_sems), Sems(recv_sems)
    started = []

    def push(src, dst, recv, device):
        copy = pltpu.make_async_remote_copy(
            src_ref=src, dst_ref=dst, send_sem=send_sems.at[ssem.take()],
            recv_sem=recv_sems.at[recv], device_id=device, device_id_type=MESH)
        copy.start()
        started.append(copy)

    def arrived(dst, recv):
        pltpu.make_async_remote_copy(
            src_ref=dst, dst_ref=dst, send_sem=send_sems.at[0],
            recv_sem=recv_sems.at[recv], device_id=sib, device_id_type=MESH).wait_recv()

    loads = [
        pltpu.make_async_copy(act.at[pl.ds(mm(c * BLK), BLK), :], a_in, load_sems.at[0]),
        pltpu.make_async_copy(cot, c_in, load_sems.at[1]),
        pltpu.make_async_copy(kept, krow, load_sems.at[2]),
        pltpu.make_async_copy(slot, srow, load_sems.at[3]),
        pltpu.make_async_copy(old, o_in, load_sems.at[4]),
    ]
    for load in loads:
        load.start()

    partners = []
    for k in range(1, NT):
        tk = (t + k) % NT
        partners.append((dp, tk))
    for k in range(1, NZ):
        zk = (z + k) % NZ
        partners.append(dev(x, c, y, zk))
        partners.append(dev(x, 1 - c, y, zk))
    partners.append(y_up)
    partners.append(y_dn)
    barrier = pltpu.get_barrier_semaphore()
    for p in partners:
        pl.semaphore_signal(barrier, inc=1, device_id=p, device_id_type=MESH)

    loads[0].wait()
    for yy in range(NY):
        for zz in range(NZ):
            ab[z, :, yy * CHUNK + zz * 128:yy * CHUNK + (zz + 1) * 128] = (
                a_in[:, (zz * NY + yy) * 128:(zz * NY + yy + 1) * 128])
    pl.semaphore_wait(barrier, len(partners))

    ring_recv = [[rsem.take(), rsem.take()] for _ in range(4)]

    def ring_rows(step, way):
        if step < 4:
            return pl.ds(0, BLK)
        return pl.ds(0, BLK // 2) if way == 0 else pl.ds(BLK // 2, BLK // 2)

    def ring_send(step):
        for way in range(2):
            block = (z + NZ - (step - 1)) % NZ if way == 0 else (z + step - 1) % NZ
            rows = ring_rows(step, way)
            push(ab.at[block, rows, :], ab.at[block, rows, :], ring_recv[step - 1][way],
                 z_up if way == 0 else z_dn)

    def ring_wait(step):
        for way in range(2):
            block = (z + NZ - step) % NZ if way == 0 else (z + step) % NZ
            arrived(ab.at[block, ring_rows(step, way), :], ring_recv[step - 1][way])

    ring_send(1)

    loads[1].wait()
    ct[...] = c_in[...].astype(F32).T.astype(BF)
    cot_recv = rsem.take(NZ * NC)
    cot_slot = cot_recv + z * NC + c
    for k in range(NZ):
        zk = (z + k) % NZ
        for e in range(NC):
            ck = (c + e) % NC
            src = ct.at[pl.ds(mm(zk * EIGHTH, 16), EIGHTH), pl.ds(mm(ck * BLK), BLK)]
            dst = cb.at[c, :, pl.ds(mm(z * BLK), BLK)]
            if k == 0 and e == 0:
                own = pltpu.make_async_copy(src, dst, load_sems.at[5])
                own.start()
                own.wait()
            else:
                push(src, dst, cot_slot, dev(x, ck, y, zk))

    loads[2].wait()
    loads[3].wait()
    kv, sv = krow[...], srow[...]
    o, j = jnp.zeros_like(kv), jnp.zeros_like(sv)
    for i in range(1, NT):
        o = o + jnp.where(kv >= ROWS * i, 1, 0)
        j = j + jnp.where(sv >= OWN * i, 1, 0)
    idx[0:1, :] = jnp.where(o == t, j, 99)
    idx[1:2, :] = jnp.where(j == t, o + 8, 99)
    row16 = iota((16, 128), 0)
    for b in range(KB):
        lanes = slice(b * 128, (b + 1) * 128)
        key = jnp.where(row16 < 8, jnp.broadcast_to(idx[0:1, lanes], (16, 128)),
                        jnp.broadcast_to(idx[1:2, lanes], (16, 128)))
        ohs[b * 16:(b + 1) * 16, :] = onehot(key == row16)
    upto = onehot(iota((128, 128), 0) <= iota((128, 128), 1))
    inc[...] = dot(ohs[...], upto)
    run = jnp.zeros((16, 1), F32)
    for b in range(KB):
        lanes = slice(b * 128, (b + 1) * 128)
        here = inc[b * 16:(b + 1) * 16, :]
        rank = ohs[b * 16:(b + 1) * 16, :].astype(F32) * (here + run)
        rank_s = jnp.sum(rank[0:8], axis=0, keepdims=True).astype(jnp.int32)
        rank_r = jnp.sum(rank[8:16], axis=0, keepdims=True).astype(jnp.int32)
        dest, source = idx[0:1, lanes], idx[1:2, lanes]
        idx[2:3, lanes] = jnp.where(dest < 99, dest * CAP + rank_s, 0)
        idx[3:4, lanes] = jnp.where(source < 99, (source - 8) * CAP + rank_r, 0)
        run = run + here[:, 127:128]
    idx[4:5, :] = kv - t * ROWS
    idx[5:6, :] = sv - t * OWN

    def scatter(step, carry):
        by_neuron, by_slot = carry
        lanes = pl.ds(mm(step * OWN), OWN)
        vs, vr, ln, ls = (idx[i:i + 1, lanes] for i in (2, 3, 4, 5))
        high = iota((32, OWN), 0) == (ln >> 7)
        values = jnp.concatenate([
            jnp.where(high, vs >> 7, 0), jnp.where(high, vs & 127, 0)], axis=0)
        low = onehot(iota((128, OWN), 0) == (ln & 127))
        by_neuron = by_neuron + dot_nt(values.astype(F32).astype(BF), low)
        high = iota((8, OWN), 0) == (ls >> 7)
        values = jnp.concatenate([
            jnp.where(high, vr >> 7, 0), jnp.where(high, vr & 127, 0)], axis=0)
        low = onehot(iota((128, OWN), 0) == (ls & 127))
        by_slot = by_slot + dot_nt(low, values.astype(F32).astype(BF))
        return by_neuron, by_slot

    by_neuron, by_slot = lax.fori_loop(
        0, KEEP // OWN, scatter, (jnp.zeros((64, 128), F32), jnp.zeros((128, 16), F32)))
    place_s = (by_neuron[0:32] * 128.0 + by_neuron[32:64]).astype(jnp.int32)
    place_r = (by_slot[:, 0:8] * 128.0 + by_slot[:, 8:16]).astype(jnp.int32)

    loads[4].wait()
    own_recv = rsem.take(NT)
    own_send = ssem.take(NT)

    def own_copy(to):
        return pltpu.make_async_remote_copy(
            src_ref=rts.at[to], dst_ref=rr.at[pl.ds(mm(t * CAP, 16), CAP), :],
            send_sem=send_sems.at[own_send + to], recv_sem=recv_sems.at[own_recv + t],
            device_id=(dp, to), device_id_type=MESH)

    def select(k, _):
        to = (t + k) % NT
        row = iota((CAP, 128), 0) + (to * CAP + 1)
        for h in range(ROWS // 128):
            pb[:, h * 128:(h + 1) * 128] = onehot(place_s[h:h + 1, :] == row)
        rts[to] = dot_nt(pb[...], o_in[...]).astype(BF)

        @pl.when(k < NT)
        def _():
            own_copy(to).start()
        return 0

    lax.fori_loop(1, NT + 1, select, 0)
    rr[pl.ds(mm(t * CAP, 16), CAP), :] = rts[t]

    ring_wait(1)
    ring_send(2)

    for k in range(1, NT):
        frm = (t + k) % NT
        arrived(rr.at[pl.ds(mm(frm * CAP, 16), CAP), :], own_recv + frm)
    pi = interleave_matrix()
    got = rr[...]
    for h in range(OWN // 128):
        q = onehot(iota((128, PLACES), 1) + 1 == place_r[:, h:h + 1])
        mine = dot(q, got).astype(BF)
        stn[h * 128:(h + 1) * 128, :] = mine
        split = dot(mine, pi).astype(BF)
        st2[0, h * 128:(h + 1) * 128, :] = split[:, 0:128]
        st2[1, h * 128:(h + 1) * 128, :] = split[:, 128:256]

    w_recv = rsem.take(NZ)
    for k in range(NZ):
        zk = (z + k) % NZ
        src = st2.at[:, pl.ds(mm(zk * EIGHTH, 16), EIGHTH), :]
        dst = wt.at[c, y, :, :, pl.ds(mm(z * 128), 128)]
        if k == 0:
            own = pltpu.make_async_copy(src, dst, load_sems.at[5])
            own.start()
            own.wait()
        else:
            push(src, dst, w_recv + z, dev(x, c, y, zk))

    stu[...] = stn[...].astype(F32).T.astype(BF)

    ring_wait(2)
    ring_send(3)

    for k in range(1, NZ):
        zk = (z + k) % NZ
        arrived(wt.at[c, y, :, :, pl.ds(mm(zk * 128), 128)], w_recv + zk)

    y1, y3, y2 = (y + 1) % NY, (y + 3) % NY, (y + 2) % NY
    wy = [rsem.take() for _ in range(4)]
    core_recv = rsem.take(NY)

    def to_core(yy):
        push(wt.at[c, yy], wt.at[c, yy], core_recv + yy, sib)

    push(wt.at[c, y], wt.at[c, y], wy[0], y_up)
    push(wt.at[c, y], wt.at[c, y], wy[1], y_dn)
    to_core(y)
    ring_wait(3)
    ring_send(4)
    arrived(wt.at[c, y3], wy[0])
    push(wt.at[c, y3, 0], wt.at[c, y3, 0], wy[2], y_up)
    arrived(wt.at[c, y1], wy[1])
    push(wt.at[c, y1, 1], wt.at[c, y1, 1], wy[3], y_dn)
    to_core(y3)
    to_core(y1)
    arrived(wt.at[c, y2, 0], wy[2])
    arrived(wt.at[c, y2, 1], wy[3])
    to_core(y2)

    for k in range(NZ):
        zk = (z + k) % NZ
        for e in range(NC):
            if k == 0 and e == 0:
                continue
            ck = (c + e) % NC
            arrived(cb.at[ck, :, pl.ds(mm(zk * BLK), BLK)], cot_recv + zk * NC + ck)
    for k in range(NY):
        yy = (y + k) % NY
        arrived(wt.at[1 - c, yy], core_recv + yy)
    ring_wait(4)

    def forward(pair, _):
        lanes = pl.ds(mm(pair * 256), 256)
        tokens = ab[pl.ds(pair * 2, 2)].reshape(256, D)
        total = jnp.zeros((448, 256), F32)
        for yy in range(NY):
            total = total + dot_nt(wt[:, yy].reshape(448, CHUNK),
                                   tokens[:, yy * CHUNK:(yy + 1) * CHUNK])
        for cc in range(NC):
            gate = total[cc * 224:cc * 224 + 112]
            up = total[cc * 224 + 112:cc * 224 + 224]
            sig = jax.nn.sigmoid(gate)
            silu = gate * sig
            hs[cc, :, lanes] = (silu * up).astype(BF)
            incoming = cb[cc, :, lanes].astype(F32)
            dg[cc, 0:112, lanes] = (incoming * up * sig * (1.0 + gate * (1.0 - sig))).astype(BF)
            dg[cc, 112:224, lanes] = (incoming * silu).astype(BF)
        return 0

    lax.fori_loop(0, NZ // 2, forward, 0)

    hid_recv = rsem.take(NZ * NC)
    for k in range(NZ):
        zk = (z + k) % NZ
        for e in range(NC):
            ck = (c + e) % NC
            src = hs.at[ck, :, pl.ds(mm(zk * BLK), BLK)]
            dst = hr.at[pl.ds(mm(z * EIGHTH, 16), EIGHTH), pl.ds(mm(c * BLK), BLK)]
            if k == 0 and e == 0:
                own = pltpu.make_async_copy(src, dst, load_sems.at[5])
                own.start()
                own.wait()
            else:
                push(src, dst, hid_recv + z * NC + c, dev(x, ck, y, zk))

    order = [y2, y1, y3, y]
    core_sum = [rsem.take() for _ in range(4)]
    for n, yy in enumerate(order):
        def part(s, _, n=n, yy=yy):
            lanes = pl.ds(mm(s * 256), 256)
            width = ab[:, :, pl.ds(mm(yy * CHUNK + s * 256), 256)].reshape(TOK, 256)
            cs[n, :, :, lanes] = dot(dg[1 - c], width).astype(BF).reshape(2, EIGHTH, 256)
            pa[n, :, :, lanes] = dot(dg[c], width).reshape(2, EIGHTH, 256)
            return 0
        lax.fori_loop(0, CHUNK // 256, part, 0)
        push(cs.at[n], cx.at[n], core_sum[n], sib)

    sem_b = [rsem.take(), rsem.take()]
    sem_c = [rsem.take(), rsem.take()]
    arrived(cx.at[0], core_sum[0])
    rb_send[...] = (pa[0] + cx[0].astype(F32)).astype(BF)
    push(rb_send.at[0], rb.at[0], sem_b[0], y_up)
    push(rb_send.at[1], rb.at[1], sem_b[1], y_dn)
    for way in range(2):
        n = 1 + way
        arrived(cx.at[n], core_sum[n])
        arrived(rb.at[way], sem_b[way])
        rc_send[way, way] = (pa[n, way] + cx[n, way].astype(F32) + rb[way].astype(F32)).astype(BF)
        rc_send[way, 1 - way] = (pa[n, 1 - way] + cx[n, 1 - way].astype(F32)).astype(BF)
        push(rc_send.at[way], rc.at[way], sem_c[way], y_up if way == 0 else y_dn)
    arrived(cx.at[3], core_sum[3])

    for k in range(NZ):
        zk = (z + k) % NZ
        for e in range(NC):
            if k == 0 and e == 0:
                continue
            ck = (c + e) % NC
            arrived(hr.at[pl.ds(mm(zk * EIGHTH, 16), EIGHTH), pl.ds(mm(ck * BLK), BLK)],
                    hid_recv + zk * NC + ck)
    hid[...] = hr[...].astype(F32).T.astype(BF)

    arrived(rc.at[0], sem_c[0])
    arrived(rc.at[1], sem_c[1])
    fg[...] = (pa[3] + cx[3].astype(F32) + rc[0].astype(F32) + rc[1].astype(F32)).astype(BF)

    g_recv = rsem.take(NZ)
    for k in range(NZ):
        zk = (z + k) % NZ
        src = fg.at[:, :, pl.ds(mm(zk * 128), 128)]
        dst = gr.at[:, pl.ds(mm(z * EIGHTH, 16), EIGHTH), :]
        if k == 0:
            own = pltpu.make_async_copy(src, dst, load_sems.at[5])
            own.start()
            own.wait()
        else:
            push(src, dst, g_recv + z, dev(x, c, y, zk))
    for k in range(1, NZ):
        zk = (z + k) % NZ
        arrived(gr.at[:, pl.ds(mm(zk * EIGHTH, 16), EIGHTH), :], g_recv + zk)
    both = jnp.concatenate([gr[0], gr[1]], axis=1)
    wg[...] = dot_nt(interleave_matrix(), both).astype(BF)

    def drain(k, _):
        own_copy((t + k) % NT).wait_send()
        return 0

    lax.fori_loop(1, NT, drain, 0)
    for copy in started:
        copy.wait_send()
    assert ssem.n <= send_sems.shape[0] and rsem.n <= recv_sems.shape[0], (ssem.n, rsem.n)


def per_device(activations, cotangent, old_gate_up, kept_index, new_slot):
    any_ = pl.BlockSpec(memory_space=pl.ANY)
    vmem = pl.BlockSpec(memory_space=pltpu.VMEM)
    V = pltpu.VMEM
    student, hidden, grad = pl.pallas_call(
        kernel,
        out_shape=(
            jax.ShapeDtypeStruct((256, OWN), BF),
            jax.ShapeDtypeStruct((256, OWN), BF),
            jax.ShapeDtypeStruct((256, OWN), BF),
        ),
        in_specs=[any_] * 5,
        out_specs=(vmem, vmem, vmem),
        scratch_shapes=[
            V((BLK, D), BF),
            V((256, OWN), BF),
            V((256, ROWS), BF),
            V((1, KEEP), jnp.int32),
            V((1, KEEP), jnp.int32),
            V((NZ, BLK, D), BF),
            V((8, KEEP), jnp.int32),
            V((KB * 16, 128), BF),
            V((KB * 16, 128), F32),
            V((CAP, ROWS), BF),
            V((NT, CAP, 256), BF),
            V((PLACES, 256), BF),
            V((OWN, 256), BF),
            V((2, OWN, 128), BF),
            V((NC, NY, 2, EIGHTH, CHUNK), BF),
            V((OWN, 256), BF),
            V((NC, EIGHTH, TOK), BF),
            V((NC, EIGHTH, TOK), BF),
            V((OWN, 256), BF),
            V((NC, 2 * EIGHTH, TOK), BF),
            V((NY, 2, EIGHTH, CHUNK), BF),
            V((NY, 2, EIGHTH, CHUNK), BF),
            V((NY, 2, EIGHTH, CHUNK), F32),
            V((2, EIGHTH, CHUNK), BF),
            V((2, EIGHTH, CHUNK), BF),
            V((2, 2, EIGHTH, CHUNK), BF),
            V((2, 2, EIGHTH, CHUNK), BF),
            V((2, EIGHTH, CHUNK), BF),
            V((2, OWN, 128), BF),
            pltpu.SemaphoreType.DMA((6,)),
            pltpu.SemaphoreType.DMA((96,)),
            pltpu.SemaphoreType.DMA((96,)),
        ],
        compiler_params=pltpu.CompilerParams(
            collective_id=0, has_side_effects=True, vmem_limit_bytes=60 * 1024 * 1024),
        cost_estimate=pl.CostEstimate(flops=12_000_000_000, bytes_accessed=8_000_000, transcendentals=1_000_000),
        name="student_projection",
    )(activations, cotangent, old_gate_up.reshape(256, ROWS),
      kept_index.reshape(1, KEEP), new_slot.reshape(1, KEEP))
    return student.reshape(128, 2, OWN), hidden, grad.reshape(128, 2, OWN)


def solution(mesh):
    placed = (P("dp", None), P("dp", "tensor"), P("dp", None, "tensor"), P(), P())
    return jax.shard_map(
        per_device,
        mesh=mesh,
        in_specs=placed,
        out_specs=(P("dp", None, "tensor"), P("dp", "tensor"), P("dp", None, "tensor")),
        check_vma=False,
    )
```

time: 854 us -> 163 us (0.19)
  waiting for transfers between devices: 588 us -> 0 us
  local copies, waits for them, and re-layouts: 174 us -> 9.69 us
  Pallas kernels: 0 us -> 152 us
  other arithmetic: 54.8 us -> 0 us
  between operations: 14.2 us -> 0.65 us
  matrix products: 12.6 us -> 0 us
    all_gather x1 -> x0, waiting for transfers between devices: 351 us -> none  [per_device(): shard_piece = lax.all_gather(student_gate_up, 'dp', axis=0, tiled=True)]
    unnamed x3 -> x0, waiting for transfers between devices: 236 us -> none
    pallas_call x0 -> x1, Pallas kernels: none -> 152 us  [per_device(): pl.pallas_call(kernel, out_shape=(jax.ShapeDtypeStruct((256, OWN), BF), j...]
    scatter x3 -> x0, local copies, waits for them, and re-layouts: 103 us -> none  [the longest x1 49.5 us: per_device(): filled = jnp.zeros((tensor_size * capacity,), jnp.bfloat16).at[target_pla...]
    another operation x4 -> x0, other arithmetic: 38.8 us -> none
    unnamed x13 -> x3, local copies, waits for them, and re-layouts: 34.3 us -> 0.77 us
    gather x4 -> x0, local copies, waits for them, and re-layouts: 18.1 us -> none  [the longest x2 10.3 us: per_device(): take_place = old_owner[my_kept] * capacity + slot_rank[my_kept]]
    all_gather x1 -> x0, local copies, waits for them, and re-layouts: 13.1 us -> none  [per_device(): shard_piece = lax.all_gather(student_gate_up, 'dp', axis=0, tiled=True)]
  transfers between devices with their start and end apart: 3 -> 0, of which waited for: 2 -> 0; matrix products, arithmetic and copies ran while one was open for 5% -> 0% of each run, Pallas kernels for 0% -> 0%
where the time goes in v1:
time: 163 us; the launch traced here: 162 us
  Pallas kernels  152 us (93%)
  local copies, waits for them, and re-layouts  9.69 us (6%)
    pallas_call x1, Pallas kernels, per_device(): pl.pallas_call(kernel, out_shape=(jax.ShapeDtypeStruct((256, OWN), BF), j...  152 us
    reshape x1, local copies, waits for them, and re-layouts, per_device(): old_gate_up.reshape(256, ROWS)  4.95 us
    reshape x2, local copies, waits for them, and re-layouts, per_device(): return (student.reshape(128, 2, OWN), hidden, grad.reshape(128, 2, OWN))  3.97 us

profile of v1, /device:TPU:32, one launch (start us, length us, event | category | flops | bytes accessed | tf_op | source)
XLA Modules:
  0.0 162.0 jit_solution(17140979867255461343)
XLA Ops:
  0.6 5.0 %reshape.21.old = bf16[256,3584]{1,0:T(8,128)(2,1)} reshape(bf16[128,2,3584]{2,1,0:T(2,128)(2,1)} %param.7) | data formatting | bytes 3670016 | tf_op jit(solution)/shard_map/reshape | solution.py:462
  5.6 151.7 %student_projection.1 = (bf16[256,896]{1,0:T(8,128)(2,1)}, bf16[256,896]{1,0:T(8,128)(2,1)}, bf16[256,896]{1,0:T(8,128)(2,1)}) custom-call(bf16[256,4096]{1,0:T(8,128)(2,1)} %act.1, bf16[256,896]{1,0:T(8,128)(2,1)} %cot.1, bf16[256,3584]{1,0:T(8,128)(2,1)} %reshape.21.old, s32[1,7168]{1,0:T(1,128)} %bitcast.2, s32[1,7168]{1,0:T(1,128)} %bitcast.3), custom_call_target="tpu_custom_call" | custom-call | flops 12000000000 | bytes 8000000 | tf_op jit(solution)/shard_map/student_projection/pallas_call | solution.py:415
  157.3 0.0 copy-start
  157.3 2.0 %reshape.24 = bf16[128,2,896]{2,1,0:T(2,128)(2,1)} reshape(bf16[256,896]{1,0:T(8,128)(2,1)} %get-tuple-element.6) | data formatting | bytes 917504 | tf_op jit(solution)/shard_map/reshape | solution.py:464
  159.3 2.0 %reshape.25 = bf16[128,2,896]{2,1,0:T(2,128)(2,1)} reshape(bf16[256,896]{1,0:T(8,128)(2,1)} %get-tuple-element.8) | data formatting | bytes 917504 | tf_op jit(solution)/shard_map/reshape | solution.py:464
  161.2 0.0 copy-done
  161.2 0.8 copy.9
Async XLA Ops:
  157.3 4.0 %copy-start = (bf16[256,896]{1,0:T(8,128)(2,1)S(1)}, bf16[256,896]{1,0:T(8,128)(2,1)}, u32[]{:S(2)}) copy-start(bf16[256,896]{1,0:T(8,128)(2,1)} %get-tuple-element.13) | copy-start | bytes 1376260

commit v2 on v1

--- a/solution.py
+++ b/solution.py
@@ -18,6 +18,9 @@
 BLK = 128
 TOK = NZ * BLK
 CHUNK = D // NY
+DIRECT = 1024
+SHARE = (D - DIRECT) // NX
+HALF = BLK // 2
 KB = KEEP // 128
 F32 = jnp.float32
 BF = jnp.bfloat16
@@ -73,6 +76,7 @@
     sib = dev(x, 1 - c, y, z)
     z_up, z_dn = dev(x, c, y, (z + 1) % NZ), dev(x, c, y, (z + NZ - 1) % NZ)
     y_up, y_dn = dev(x, c, (y + 1) % NY, z), dev(x, c, (y + NY - 1) % NY, z)
+    x_up, x_dn = dev((x + 1) % NX, c, y, z), dev((x + NX - 1) % NX, c, y, z)
 
     ssem, rsem = Sems(send_sems), Sems(recv_sems)
     started = []
@@ -120,26 +124,64 @@
                 a_in[:, (zz * NY + yy) * 128:(zz * NY + yy + 1) * 128])
     pl.semaphore_wait(barrier, len(partners))
 
-    ring_recv = [[rsem.take(), rsem.take()] for _ in range(4)]
+    def share(xx):
+        return pl.ds(mm(DIRECT + xx % NX * SHARE), SHARE)
+
+    regions = [share(x), pl.ds(0, DIRECT)]
+    ring_recv = [[[rsem.take(), rsem.take()] for _ in range(2)] for _ in range(4)]
+    hand_recv = [[rsem.take(4), rsem.take(4)] for _ in range(4)]
+
+    def ring_block(step, way):
+        return (z + NZ - step) % NZ if way == 0 else (z + step) % NZ
 
     def ring_rows(step, way):
         if step < 4:
             return pl.ds(0, BLK)
-        return pl.ds(0, BLK // 2) if way == 0 else pl.ds(BLK // 2, BLK // 2)
-
-    def ring_send(step):
+        return pl.ds(0, HALF) if way == 0 else pl.ds(HALF, HALF)
+
+    def ring_send(step, r):
         for way in range(2):
-            block = (z + NZ - (step - 1)) % NZ if way == 0 else (z + step - 1) % NZ
-            rows = ring_rows(step, way)
-            push(ab.at[block, rows, :], ab.at[block, rows, :], ring_recv[step - 1][way],
-                 z_up if way == 0 else z_dn)
-
-    def ring_wait(step):
+            piece = ab.at[ring_block(step - 1, way), ring_rows(step, way), regions[r]]
+            push(piece, piece, ring_recv[step - 1][way][r], z_up if way == 0 else z_dn)
+
+    def ring_wait(step, r):
         for way in range(2):
-            block = (z + NZ - step) % NZ if way == 0 else (z + step) % NZ
-            arrived(ab.at[block, ring_rows(step, way), :], ring_recv[step - 1][way])
-
-    ring_send(1)
+            arrived(ab.at[ring_block(step, way), ring_rows(step, way), regions[r]],
+                    ring_recv[step - 1][way][r])
+
+    def hand_blocks(step):
+        return [(ring_block(step, way), hand_recv[step - 1][way]) for way in range(2 if step < 4 else 1)]
+
+    def hand_on(step):
+        for block, sem in hand_blocks(step):
+            piece = ab.at[block, :, share(x)]
+            push(piece, piece, sem, x_up)
+            push(piece, piece, sem + 1, x_dn)
+
+    def relay(step):
+        for block, sem in hand_blocks(step):
+            arrived(ab.at[block, :, share(x + 3)], sem)
+            piece = ab.at[block, pl.ds(0, HALF), share(x + 3)]
+            push(piece, piece, sem + 2, x_up)
+            arrived(ab.at[block, :, share(x + 1)], sem + 1)
+            piece = ab.at[block, pl.ds(HALF, HALF), share(x + 1)]
+            push(piece, piece, sem + 3, x_dn)
+
+    def handed(step):
+        for block, sem in hand_blocks(step):
+            arrived(ab.at[block, pl.ds(0, HALF), share(x + 2)], sem + 2)
+            arrived(ab.at[block, pl.ds(HALF, HALF), share(x + 2)], sem + 3)
+
+    def ring(step):
+        for r in range(2):
+            ring_wait(step, r)
+            if step < 4:
+                ring_send(step + 1, r)
+            if r == 0:
+                hand_on(step)
+
+    ring_send(1, 0)
+    ring_send(1, 1)
 
     loads[1].wait()
     ct[...] = c_in[...].astype(F32).T.astype(BF)
@@ -235,8 +277,7 @@
     lax.fori_loop(1, NT + 1, select, 0)
     rr[pl.ds(mm(t * CAP, 16), CAP), :] = rts[t]
 
-    ring_wait(1)
-    ring_send(2)
+    ring(1)
 
     for k in range(1, NT):
         frm = (t + k) % NT
@@ -252,47 +293,59 @@
         st2[1, h * 128:(h + 1) * 128, :] = split[:, 128:256]
 
     w_recv = rsem.take(NZ)
-    for k in range(NZ):
-        zk = (z + k) % NZ
-        src = st2.at[:, pl.ds(mm(zk * EIGHTH, 16), EIGHTH), :]
-        dst = wt.at[c, y, :, :, pl.ds(mm(z * 128), 128)]
-        if k == 0:
-            own = pltpu.make_async_copy(src, dst, load_sems.at[5])
-            own.start()
-            own.wait()
-        else:
-            push(src, dst, w_recv + z, dev(x, c, y, zk))
+
+    def eighth(k):
+        zk = (z + k) % NZ
+        return (st2.at[:, pl.ds(mm(zk * EIGHTH, 16), EIGHTH), :],
+                wt.at[c, y, :, :, pl.ds(mm(z * 128), 128)], dev(x, c, y, zk))
+
+    own = pltpu.make_async_copy(*eighth(0)[:2], load_sems.at[5])
+    own.start()
+    for k in (1, 7, 2, 6, 3, 5, 4):
+        src, dst, to = eighth(k)
+        push(src, dst, w_recv + z, to)
+    own.wait()
 
     stu[...] = stn[...].astype(F32).T.astype(BF)
 
-    ring_wait(2)
-    ring_send(3)
-
-    for k in range(1, NZ):
-        zk = (z + k) % NZ
-        arrived(wt.at[c, y, :, :, pl.ds(mm(zk * 128), 128)], w_recv + zk)
+    relay(1)
+    ring(2)
 
     y1, y3, y2 = (y + 1) % NY, (y + 3) % NY, (y + 2) % NY
-    wy = [rsem.take() for _ in range(4)]
-    core_recv = rsem.take(NY)
-
-    def to_core(yy):
-        push(wt.at[c, yy], wt.at[c, yy], core_recv + yy, sib)
-
-    push(wt.at[c, y], wt.at[c, y], wy[0], y_up)
-    push(wt.at[c, y], wt.at[c, y], wy[1], y_dn)
-    to_core(y)
-    ring_wait(3)
-    ring_send(4)
-    arrived(wt.at[c, y3], wy[0])
-    push(wt.at[c, y3, 0], wt.at[c, y3, 0], wy[2], y_up)
-    arrived(wt.at[c, y1], wy[1])
-    push(wt.at[c, y1, 1], wt.at[c, y1, 1], wy[3], y_dn)
-    to_core(y3)
-    to_core(y1)
-    arrived(wt.at[c, y2, 0], wy[2])
-    arrived(wt.at[c, y2, 1], wy[3])
-    to_core(y2)
+    pairs = [(z // 2 + k) % (NZ // 2) for k in (0, 1, 3, 2)]
+    wy = [rsem.take(4) for _ in pairs]
+    core_recv = rsem.take(NY * len(pairs))
+
+    def w_part(cc, yy, pair):
+        return wt.at[cc, yy, :, :, pl.ds(mm(pair * 256, 256), 256)]
+
+    def w_half(yy, g, pair):
+        return wt.at[c, yy, g, :, pl.ds(mm(pair * 256, 256), 256)]
+
+    def to_core(yy, pair):
+        push(w_part(c, yy, pair), w_part(c, yy, pair), core_recv + pair * NY + yy, sib)
+
+    for n, pair in enumerate(pairs):
+        for zk in ([z + 1 - 2 * (z % 2)] if n == 0 else [pair * 2, pair * 2 + 1]):
+            arrived(wt.at[c, y, :, :, pl.ds(mm(zk * 128), 128)], w_recv + zk)
+        push(w_part(c, y, pair), w_part(c, y, pair), wy[n], y_up)
+        push(w_part(c, y, pair), w_part(c, y, pair), wy[n] + 1, y_dn)
+        to_core(y, pair)
+    relay(2)
+    ring(3)
+    for n, pair in enumerate(pairs):
+        arrived(w_part(c, y3, pair), wy[n])
+        push(w_half(y3, 0, pair), w_half(y3, 0, pair), wy[n] + 2, y_up)
+        arrived(w_part(c, y1, pair), wy[n] + 1)
+        push(w_half(y1, 1, pair), w_half(y1, 1, pair), wy[n] + 3, y_dn)
+        to_core(y3, pair)
+        to_core(y1, pair)
+    relay(3)
+    for n, pair in enumerate(pairs):
+        arrived(w_half(y2, 0, pair), wy[n] + 2)
+        arrived(w_half(y2, 1, pair), wy[n] + 3)
+        to_core(y2, pair)
+    ring(4)
 
     for k in range(NZ):
         zk = (z + k) % NZ
@@ -301,33 +354,31 @@
                 continue
             ck = (c + e) % NC
             arrived(cb.at[ck, :, pl.ds(mm(zk * BLK), BLK)], cot_recv + zk * NC + ck)
-    for k in range(NY):
-        yy = (y + k) % NY
-        arrived(wt.at[1 - c, yy], core_recv + yy)
-    ring_wait(4)
-
-    def forward(pair, _):
-        lanes = pl.ds(mm(pair * 256), 256)
-        tokens = ab[pl.ds(pair * 2, 2)].reshape(256, D)
+    for pair in pairs:
+        for yy in (y, y3, y1, y2):
+            arrived(w_part(1 - c, yy, pair), core_recv + pair * NY + yy)
+
+    hid_recv = rsem.take(NZ * NC)
+
+    def forward(blocks):
+        tokens = jnp.concatenate([ab[b] for b in blocks], axis=0)
         total = jnp.zeros((448, 256), F32)
         for yy in range(NY):
             total = total + dot_nt(wt[:, yy].reshape(448, CHUNK),
                                    tokens[:, yy * CHUNK:(yy + 1) * CHUNK])
         for cc in range(NC):
-            gate = total[cc * 224:cc * 224 + 112]
-            up = total[cc * 224 + 112:cc * 224 + 224]
-            sig = jax.nn.sigmoid(gate)
-            silu = gate * sig
-            hs[cc, :, lanes] = (silu * up).astype(BF)
-            incoming = cb[cc, :, lanes].astype(F32)
-            dg[cc, 0:112, lanes] = (incoming * up * sig * (1.0 + gate * (1.0 - sig))).astype(BF)
-            dg[cc, 112:224, lanes] = (incoming * silu).astype(BF)
-        return 0
-
-    lax.fori_loop(0, NZ // 2, forward, 0)
-
-    hid_recv = rsem.take(NZ * NC)
-    for k in range(NZ):
+            for i, b in enumerate(blocks):
+                lanes = pl.ds(mm(b * BLK), BLK)
+                gate = total[cc * 224:cc * 224 + 112, i * BLK:(i + 1) * BLK]
+                up = total[cc * 224 + 112:cc * 224 + 224, i * BLK:(i + 1) * BLK]
+                sig = jax.nn.sigmoid(gate)
+                silu = gate * sig
+                hs[cc, :, lanes] = (silu * up).astype(BF)
+                incoming = cb[cc, :, lanes].astype(F32)
+                dg[cc, 0:112, lanes] = (incoming * up * sig * (1.0 + gate * (1.0 - sig))).astype(BF)
+                dg[cc, 112:224, lanes] = (incoming * silu).astype(BF)
+
+    def hidden_out(k):
         zk = (z + k) % NZ
         for e in range(NC):
             ck = (c + e) % NC
@@ -340,32 +391,87 @@
             else:
                 push(src, dst, hid_recv + z * NC + c, dev(x, ck, y, zk))
 
+    for step in (1, 2, 3):
+        handed(step)
+        forward([ring_block(step, 0), ring_block(step, 1)])
+        hidden_out(NZ - step)
+        hidden_out(step)
+        if step == 2:
+            relay(4)
+    handed(4)
+    forward([z, ring_block(4, 0)])
+    hidden_out(4)
+    hidden_out(0)
+
     order = [y2, y1, y3, y]
-    core_sum = [rsem.take() for _ in range(4)]
-    for n, yy in enumerate(order):
-        def part(s, _, n=n, yy=yy):
-            lanes = pl.ds(mm(s * 256), 256)
-            width = ab[:, :, pl.ds(mm(yy * CHUNK + s * 256), 256)].reshape(TOK, 256)
-            cs[n, :, :, lanes] = dot(dg[1 - c], width).astype(BF).reshape(2, EIGHTH, 256)
-            pa[n, :, :, lanes] = dot(dg[c], width).reshape(2, EIGHTH, 256)
-            return 0
-        lax.fori_loop(0, CHUNK // 256, part, 0)
-        push(cs.at[n], cx.at[n], core_sum[n], sib)
-
-    sem_b = [rsem.take(), rsem.take()]
-    sem_c = [rsem.take(), rsem.take()]
-    arrived(cx.at[0], core_sum[0])
-    rb_send[...] = (pa[0] + cx[0].astype(F32)).astype(BF)
-    push(rb_send.at[0], rb.at[0], sem_b[0], y_up)
-    push(rb_send.at[1], rb.at[1], sem_b[1], y_dn)
-    for way in range(2):
-        n = 1 + way
-        arrived(cx.at[n], core_sum[n])
-        arrived(rb.at[way], sem_b[way])
-        rc_send[way, way] = (pa[n, way] + cx[n, way].astype(F32) + rb[way].astype(F32)).astype(BF)
-        rc_send[way, 1 - way] = (pa[n, 1 - way] + cx[n, 1 - way].astype(F32)).astype(BF)
-        push(rc_send.at[way], rc.at[way], sem_c[way], y_up if way == 0 else y_dn)
-    arrived(cx.at[3], core_sum[3])
+    parts = [(z // 2 + k) % (NZ // 2) for k in (2, 1, 3, 0)]
+    core_sum = [[rsem.take() for _ in order] for _ in parts]
+    sem_b = [[rsem.take(), rsem.take()] for _ in parts]
+    sem_c = [[rsem.take(), rsem.take()] for _ in parts]
+    g_recv = rsem.take(NZ)
+
+    def lanes_of(pair):
+        return pl.ds(mm(pair * 256, 256), 256)
+
+    def gradient(p):
+        for n, yy in enumerate(order):
+            width = ab[:, :, pl.ds(mm(yy * CHUNK + parts[p] * 256, 256), 256)].reshape(TOK, 256)
+            cs[p, n] = dot(dg[1 - c], width).astype(BF).reshape(2, EIGHTH, 256)
+            push(cs.at[p, n], cx.at[p, n], core_sum[p][n], sib)
+            pa[p, n] = dot(dg[c], width).reshape(2, EIGHTH, 256)
+
+    def send_b(p):
+        arrived(cx.at[p, 0], core_sum[p][0])
+        rb_send[p] = (pa[p, 0] + cx[p, 0].astype(F32)).astype(BF)
+        push(rb_send.at[p, 0], rb.at[p, 0], sem_b[p][0], y_up)
+        push(rb_send.at[p, 1], rb.at[p, 1], sem_b[p][1], y_dn)
+
+    def send_c(p):
+        for way in range(2):
+            n = 1 + way
+            arrived(cx.at[p, n], core_sum[p][n])
+            rc_send[p, way, 1 - way] = (pa[p, n, 1 - way] + cx[p, n, 1 - way].astype(F32)).astype(BF)
+            arrived(rb.at[p, way], sem_b[p][way])
+            rc_send[p, way, way] = (
+                pa[p, n, way] + cx[p, n, way].astype(F32) + rb[p, way].astype(F32)).astype(BF)
+            push(rc_send.at[p, way], rc.at[p, way], sem_c[p][way], y_up if way == 0 else y_dn)
+
+    def send_g(p):
+        arrived(cx.at[p, 3], core_sum[p][3])
+        total = pa[p, 3] + cx[p, 3].astype(F32)
+        for way in range(2):
+            arrived(rc.at[p, way], sem_c[p][way])
+            total = total + rc[p, way].astype(F32)
+        fg[:, :, lanes_of(parts[p])] = total.astype(BF)
+        for i in range(2):
+            zk = parts[p] * 2 + i
+            src = fg.at[:, :, pl.ds(mm(zk * 128), 128)]
+            dst = gr.at[:, pl.ds(mm(z * EIGHTH, 16), EIGHTH), :]
+            if p < 3:
+                push(src, dst, g_recv + z, dev(x, c, y, zk))
+        if p == 3:
+            zk = z + 1 - 2 * (z % 2)
+            push(fg.at[:, :, pl.ds(mm(zk * 128), 128)],
+                 gr.at[:, pl.ds(mm(z * EIGHTH, 16), EIGHTH), :], g_recv + z, dev(x, c, y, zk))
+            own = pltpu.make_async_copy(fg.at[:, :, pl.ds(mm(z * 128), 128)],
+                                        gr.at[:, pl.ds(mm(z * EIGHTH, 16), EIGHTH), :], load_sems.at[5])
+            own.start()
+            own.wait()
+
+    gradient(0)
+    gradient(1)
+    send_b(0)
+    gradient(2)
+    send_b(1)
+    send_c(0)
+    gradient(3)
+    send_b(2)
+    send_c(1)
+    send_g(0)
+    send_b(3)
+    send_c(2)
+    send_g(1)
+    send_c(3)
 
     for k in range(NZ):
         zk = (z + k) % NZ
@@ -377,21 +483,8 @@
                     hid_recv + zk * NC + ck)
     hid[...] = hr[...].astype(F32).T.astype(BF)
 
-    arrived(rc.at[0], sem_c[0])
-    arrived(rc.at[1], sem_c[1])
-    fg[...] = (pa[3] + cx[3].astype(F32) + rc[0].astype(F32) + rc[1].astype(F32)).astype(BF)
-
-    g_recv = rsem.take(NZ)
-    for k in range(NZ):
-        zk = (z + k) % NZ
-        src = fg.at[:, :, pl.ds(mm(zk * 128), 128)]
-        dst = gr.at[:, pl.ds(mm(z * EIGHTH, 16), EIGHTH), :]
-        if k == 0:
-            own = pltpu.make_async_copy(src, dst, load_sems.at[5])
-            own.start()
-            own.wait()
-        else:
-            push(src, dst, g_recv + z, dev(x, c, y, zk))
+    send_g(2)
+    send_g(3)
     for k in range(1, NZ):
         zk = (z + k) % NZ
         arrived(gr.at[:, pl.ds(mm(zk * EIGHTH, 16), EIGHTH), :], g_recv + zk)
@@ -442,18 +535,18 @@
             V((NC, EIGHTH, TOK), BF),
             V((OWN, 256), BF),
             V((NC, 2 * EIGHTH, TOK), BF),
-            V((NY, 2, EIGHTH, CHUNK), BF),
-            V((NY, 2, EIGHTH, CHUNK), BF),
-            V((NY, 2, EIGHTH, CHUNK), F32),
-            V((2, EIGHTH, CHUNK), BF),
-            V((2, EIGHTH, CHUNK), BF),
-            V((2, 2, EIGHTH, CHUNK), BF),
-            V((2, 2, EIGHTH, CHUNK), BF),
+            V((4, NY, 2, EIGHTH, 256), BF),
+            V((4, NY, 2, EIGHTH, 256), BF),
+            V((4, NY, 2, EIGHTH, 256), F32),
+            V((4, 2, EIGHTH, 256), BF),
+            V((4, 2, EIGHTH, 256), BF),
+            V((4, 2, 2, EIGHTH, 256), BF),
+            V((4, 2, 2, EIGHTH, 256), BF),
             V((2, EIGHTH, CHUNK), BF),
             V((2, OWN, 128), BF),
             pltpu.SemaphoreType.DMA((6,)),
-            pltpu.SemaphoreType.DMA((96,)),
-            pltpu.SemaphoreType.DMA((96,)),
+            pltpu.SemaphoreType.DMA((224,)),
+            pltpu.SemaphoreType.DMA((224,)),
         ],
         compiler_params=pltpu.CompilerParams(
             collective_id=0, has_side_effects=True, vmem_limit_bytes=60 * 1024 * 1024),

time: 163 us -> 122 us (0.75)
  Pallas kernels: 152 us -> 110 us
    pallas_call x1, Pallas kernels: 152 us -> 110 us  [per_device(): pl.pallas_call(kernel, out_shape=(jax.ShapeDtypeStruct((256, OWN), BF), j...]
where the time goes in v2:
time: 122 us; the launch traced here: 121 us
  Pallas kernels  110 us (90%)
  local copies, waits for them, and re-layouts  9.69 us (8%)
    pallas_call x1, Pallas kernels, per_device(): pl.pallas_call(kernel, out_shape=(jax.ShapeDtypeStruct((256, OWN), BF), j...  110 us
    reshape x1, local copies, waits for them, and re-layouts, per_device(): old_gate_up.reshape(256, ROWS)  4.95 us
    reshape x2, local copies, waits for them, and re-layouts, per_device(): return (student.reshape(128, 2, OWN), hidden, grad.reshape(128, 2, OWN))  3.97 us

profile of v2, /device:TPU:32, one launch (start us, length us, event | category | flops | bytes accessed | tf_op | source)
XLA Modules:
  0.0 120.7 jit_solution(17633172639027427524)
XLA Ops:
  0.6 5.0 %reshape.21.old = bf16[256,3584]{1,0:T(8,128)(2,1)} reshape(bf16[128,2,3584]{2,1,0:T(2,128)(2,1)} %param.7) | data formatting | bytes 3670016 | tf_op jit(solution)/shard_map/reshape | solution.py:555
  5.6 110.3 %student_projection.1 = (bf16[256,896]{1,0:T(8,128)(2,1)}, bf16[256,896]{1,0:T(8,128)(2,1)}, bf16[256,896]{1,0:T(8,128)(2,1)}) custom-call(bf16[256,4096]{1,0:T(8,128)(2,1)} %act.1, bf16[256,896]{1,0:T(8,128)(2,1)} %cot.1, bf16[256,3584]{1,0:T(8,128)(2,1)} %reshape.21.old, s32[1,7168]{1,0:T(1,128)} %bitcast.2, s32[1,7168]{1,0:T(1,128)} %bitcast.3), custom_call_target="tpu_custom_call" | custom-call | flops 12000000000 | bytes 8000000 | tf_op jit(solution)/shard_map/student_projection/pallas_call | solution.py:508
  115.9 0.0 copy-start
  115.9 2.0 %reshape.24 = bf16[128,2,896]{2,1,0:T(2,128)(2,1)} reshape(bf16[256,896]{1,0:T(8,128)(2,1)} %get-tuple-element.6) | data formatting | bytes 917504 | tf_op jit(solution)/shard_map/reshape | solution.py:557
  117.9 2.0 %reshape.25 = bf16[128,2,896]{2,1,0:T(2,128)(2,1)} reshape(bf16[256,896]{1,0:T(8,128)(2,1)} %get-tuple-element.8) | data formatting | bytes 917504 | tf_op jit(solution)/shard_map/reshape | solution.py:557
  119.9 0.0 copy-done
  119.9 0.8 copy.9
Async XLA Ops:
  115.9 4.0 %copy-start = (bf16[256,896]{1,0:T(8,128)(2,1)S(1)}, bf16[256,896]{1,0:T(8,128)(2,1)}, u32[]{:S(2)}) copy-start(bf16[256,896]{1,0:T(8,128)(2,1)} %get-tuple-element.13) | copy-start | bytes 1376260

commit v3 on v2

--- a/solution.py
+++ b/solution.py
@@ -61,9 +61,30 @@
         return first
 
 
-def kernel(act, cot, old, kept, slot, stu, hid, wg,
-           a_in, c_in, o_in, krow, srow, ab, idx, ohs, inc, pb, rts, rr, stn, st2, wt, ct, cb,
-           hs, hr, dg, cs, cx, pa, rb_send, rb, rc_send, rc, fg, gr,
+def finish(stn, hr, gr, stu, hid, wg, stn_v, hr_v, gr_v, stu_v, hid_v, wg_v, sems):
+    loads = [pltpu.make_async_copy(a, b, sems.at[i])
+             for i, (a, b) in enumerate(((stn, stn_v), (hr, hr_v), (gr, gr_v)))]
+    stores = [pltpu.make_async_copy(a, b, sems.at[i + 3])
+              for i, (a, b) in enumerate(((stu_v, stu), (hid_v, hid), (wg_v, wg)))]
+    for load in loads:
+        load.start()
+    loads[0].wait()
+    stu_v[...] = stn_v[...].astype(F32).T.astype(BF).reshape(128, 2, OWN)
+    stores[0].start()
+    loads[1].wait()
+    hid_v[...] = hr_v[...].astype(F32).T.astype(BF)
+    stores[1].start()
+    loads[2].wait()
+    both = jnp.concatenate([gr_v[0], gr_v[1]], axis=1)
+    wg_v[...] = dot_nt(interleave_matrix(), both).astype(BF).reshape(128, 2, OWN)
+    stores[2].start()
+    for store in stores:
+        store.wait()
+
+
+def kernel(act, cot, old, kept, slot, stn, hr, gr,
+           a_in, c_in, o_in, o_two, krow, srow, ab, idx, ohs, inc, pb, rts, rr, st2, wt, ct, cb,
+           hs, gu, dg, cs, cx, pa, rb_send, rb, rc_send, rc, fg,
            load_sems, send_sems, recv_sems):
     dp = lax.axis_index("dp")
     t = lax.axis_index("tensor")
@@ -92,16 +113,6 @@
         pltpu.make_async_remote_copy(
             src_ref=dst, dst_ref=dst, send_sem=send_sems.at[0],
             recv_sem=recv_sems.at[recv], device_id=sib, device_id_type=MESH).wait_recv()
-
-    loads = [
-        pltpu.make_async_copy(act.at[pl.ds(mm(c * BLK), BLK), :], a_in, load_sems.at[0]),
-        pltpu.make_async_copy(cot, c_in, load_sems.at[1]),
-        pltpu.make_async_copy(kept, krow, load_sems.at[2]),
-        pltpu.make_async_copy(slot, srow, load_sems.at[3]),
-        pltpu.make_async_copy(old, o_in, load_sems.at[4]),
-    ]
-    for load in loads:
-        load.start()
 
     partners = []
     for k in range(1, NT):
@@ -117,12 +128,21 @@
     for p in partners:
         pl.semaphore_signal(barrier, inc=1, device_id=p, device_id_type=MESH)
 
+    loads = [
+        pltpu.make_async_copy(act.at[pl.ds(mm(c * BLK), BLK), :], a_in, load_sems.at[0]),
+        pltpu.make_async_copy(cot, c_in, load_sems.at[1]),
+        pltpu.make_async_copy(kept, krow, load_sems.at[2]),
+        pltpu.make_async_copy(slot, srow, load_sems.at[3]),
+        pltpu.make_async_copy(old, o_in, load_sems.at[4]),
+    ]
+    for load in loads:
+        load.start()
+
     loads[0].wait()
     for yy in range(NY):
         for zz in range(NZ):
             ab[z, :, yy * CHUNK + zz * 128:yy * CHUNK + (zz + 1) * 128] = (
                 a_in[:, (zz * NY + yy) * 128:(zz * NY + yy + 1) * 128])
-    pl.semaphore_wait(barrier, len(partners))
 
     def share(xx):
         return pl.ds(mm(DIRECT + xx % NX * SHARE), SHARE)
@@ -172,33 +192,36 @@
             arrived(ab.at[block, pl.ds(0, HALF), share(x + 2)], sem + 2)
             arrived(ab.at[block, pl.ds(HALF, HALF), share(x + 2)], sem + 3)
 
-    def ring(step):
-        for r in range(2):
-            ring_wait(step, r)
-            if step < 4:
-                ring_send(step + 1, r)
-            if r == 0:
-                hand_on(step)
-
-    ring_send(1, 0)
-    ring_send(1, 1)
+    def ring(step, r):
+        ring_wait(step, r)
+        if step < 4:
+            ring_send(step + 1, r)
+        if r == 0:
+            hand_on(step)
 
     loads[1].wait()
     ct[...] = c_in[...].astype(F32).T.astype(BF)
     cot_recv = rsem.take(NZ * NC)
     cot_slot = cot_recv + z * NC + c
-    for k in range(NZ):
-        zk = (z + k) % NZ
-        for e in range(NC):
-            ck = (c + e) % NC
-            src = ct.at[pl.ds(mm(zk * EIGHTH, 16), EIGHTH), pl.ds(mm(ck * BLK), BLK)]
-            dst = cb.at[c, :, pl.ds(mm(z * BLK), BLK)]
-            if k == 0 and e == 0:
-                own = pltpu.make_async_copy(src, dst, load_sems.at[5])
-                own.start()
-                own.wait()
-            else:
-                push(src, dst, cot_slot, dev(x, ck, y, zk))
+
+    def cot_push(k, e):
+        zk, ck = (z + k) % NZ, (c + e) % NC
+        src = ct.at[pl.ds(mm(zk * EIGHTH, 16), EIGHTH), pl.ds(mm(ck * BLK), BLK)]
+        dst = cb.at[c, :, pl.ds(mm(z * BLK), BLK)]
+        if k == 0 and e == 0:
+            own = pltpu.make_async_copy(src, dst, load_sems.at[5])
+            own.start()
+            own.wait()
+        else:
+            push(src, dst, cot_slot, dev(x, ck, y, zk))
+
+    def both_ways(k):
+        return (k, NZ - k) if k < 4 else (4,)
+
+    def cot_out(distance):
+        for k in both_ways(distance):
+            for e in range(NC):
+                cot_push(k, e)
 
     loads[2].wait()
     loads[3].wait()
@@ -253,6 +276,11 @@
     place_r = (by_slot[:, 0:8] * 128.0 + by_slot[:, 8:16]).astype(jnp.int32)
 
     loads[4].wait()
+    o_two[...] = o_in[...].reshape(256, ROWS)
+
+    pl.semaphore_wait(barrier, len(partners))
+    ring_send(1, 0)
+    ring_send(1, 1)
     own_recv = rsem.take(NT)
     own_send = ssem.take(NT)
 
@@ -267,18 +295,21 @@
         row = iota((CAP, 128), 0) + (to * CAP + 1)
         for h in range(ROWS // 128):
             pb[:, h * 128:(h + 1) * 128] = onehot(place_s[h:h + 1, :] == row)
-        rts[to] = dot_nt(pb[...], o_in[...]).astype(BF)
-
-        @pl.when(k < NT)
-        def _():
-            own_copy(to).start()
+        rts[to] = dot_nt(pb[...], o_two[...]).astype(BF)
         return 0
 
-    lax.fori_loop(1, NT + 1, select, 0)
+    lax.fori_loop(0, NT, select, 0)
+
+    def own_start(k, _):
+        own_copy((t + k) % NT).start()
+        return 0
+
+    lax.fori_loop(1, NT, own_start, 0)
     rr[pl.ds(mm(t * CAP, 16), CAP), :] = rts[t]
 
-    ring(1)
-
+    cot_out(4)
+    cot_push(0, 1)
+    ring(1, 0)
     for k in range(1, NT):
         frm = (t + k) % NT
         arrived(rr.at[pl.ds(mm(frm * CAP, 16), CAP), :], own_recv + frm)
@@ -301,15 +332,12 @@
 
     own = pltpu.make_async_copy(*eighth(0)[:2], load_sems.at[5])
     own.start()
-    for k in (1, 7, 2, 6, 3, 5, 4):
-        src, dst, to = eighth(k)
-        push(src, dst, w_recv + z, to)
     own.wait()
 
-    stu[...] = stn[...].astype(F32).T.astype(BF)
-
-    relay(1)
-    ring(2)
+    def w_out(distance):
+        for k in both_ways(distance):
+            src, dst, to = eighth(k)
+            push(src, dst, w_recv + z, to)
 
     y1, y3, y2 = (y + 1) % NY, (y + 3) % NY, (y + 2) % NY
     pairs = [(z // 2 + k) % (NZ // 2) for k in (0, 1, 3, 2)]
@@ -325,38 +353,33 @@
     def to_core(yy, pair):
         push(w_part(c, yy, pair), w_part(c, yy, pair), core_recv + pair * NY + yy, sib)
 
-    for n, pair in enumerate(pairs):
+    def w_round(n):
+        pair = pairs[n]
         for zk in ([z + 1 - 2 * (z % 2)] if n == 0 else [pair * 2, pair * 2 + 1]):
             arrived(wt.at[c, y, :, :, pl.ds(mm(zk * 128), 128)], w_recv + zk)
         push(w_part(c, y, pair), w_part(c, y, pair), wy[n], y_up)
         push(w_part(c, y, pair), w_part(c, y, pair), wy[n] + 1, y_dn)
         to_core(y, pair)
-    relay(2)
-    ring(3)
-    for n, pair in enumerate(pairs):
+
+    def w_relay(n):
+        pair = pairs[n]
         arrived(w_part(c, y3, pair), wy[n])
         push(w_half(y3, 0, pair), w_half(y3, 0, pair), wy[n] + 2, y_up)
         arrived(w_part(c, y1, pair), wy[n] + 1)
         push(w_half(y1, 1, pair), w_half(y1, 1, pair), wy[n] + 3, y_dn)
         to_core(y3, pair)
         to_core(y1, pair)
-    relay(3)
-    for n, pair in enumerate(pairs):
+
+    def w_last(n):
+        pair = pairs[n]
         arrived(w_half(y2, 0, pair), wy[n] + 2)
         arrived(w_half(y2, 1, pair), wy[n] + 3)
         to_core(y2, pair)
-    ring(4)
-
-    for k in range(NZ):
-        zk = (z + k) % NZ
-        for e in range(NC):
-            if k == 0 and e == 0:
-                continue
-            ck = (c + e) % NC
-            arrived(cb.at[ck, :, pl.ds(mm(zk * BLK), BLK)], cot_recv + zk * NC + ck)
-    for pair in pairs:
-        for yy in (y, y3, y1, y2):
-            arrived(w_part(1 - c, yy, pair), core_recv + pair * NY + yy)
+
+    def w_from_core():
+        for pair in pairs:
+            for yy in (y, y3, y1, y2):
+                arrived(w_part(1 - c, yy, pair), core_recv + pair * NY + yy)
 
     hid_recv = rsem.take(NZ * NC)
 
@@ -371,9 +394,17 @@
                 lanes = pl.ds(mm(b * BLK), BLK)
                 gate = total[cc * 224:cc * 224 + 112, i * BLK:(i + 1) * BLK]
                 up = total[cc * 224 + 112:cc * 224 + 224, i * BLK:(i + 1) * BLK]
+                gu[cc, 0, :, lanes] = gate
+                gu[cc, 1, :, lanes] = up
+                hs[cc, :, lanes] = (gate * jax.nn.sigmoid(gate) * up).astype(BF)
+
+    def backward(blocks):
+        for cc in range(NC):
+            for b in blocks:
+                lanes = pl.ds(mm(b * BLK), BLK)
+                gate, up = gu[cc, 0, :, lanes], gu[cc, 1, :, lanes]
                 sig = jax.nn.sigmoid(gate)
                 silu = gate * sig
-                hs[cc, :, lanes] = (silu * up).astype(BF)
                 incoming = cb[cc, :, lanes].astype(F32)
                 dg[cc, 0:112, lanes] = (incoming * up * sig * (1.0 + gate * (1.0 - sig))).astype(BF)
                 dg[cc, 112:224, lanes] = (incoming * silu).astype(BF)
@@ -391,18 +422,63 @@
             else:
                 push(src, dst, hid_recv + z * NC + c, dev(x, ck, y, zk))
 
-    for step in (1, 2, 3):
-        handed(step)
-        forward([ring_block(step, 0), ring_block(step, 1)])
-        hidden_out(NZ - step)
-        hidden_out(step)
-        if step == 2:
-            relay(4)
+    def blocks_of(step):
+        return [ring_block(step, 0), ring_block(step, 1) if step < 4 else z]
+
+    def cot_in():
+        cot_push(0, 0)
+        for k in range(NZ):
+            zk = (z + k) % NZ
+            for e in range(NC):
+                if k == 0 and e == 0:
+                    continue
+                ck = (c + e) % NC
+                arrived(cb.at[ck, :, pl.ds(mm(zk * BLK), BLK)], cot_recv + zk * NC + ck)
+
+    w_out(3)
+    w_out(1)
+    ring(2, 0)
+    w_out(2)
+    w_round(2)
+    w_round(0)
+    relay(1)
+    ring(1, 1)
+    w_out(4)
+    ring(3, 0)
+    w_relay(0)
+    ring(4, 0)
+    ring(2, 1)
+    w_relay(2)
+    cot_out(1)
+    relay(2)
+    cot_out(2)
+    w_last(0)
+    w_round(3)
+    w_last(2)
+    w_round(1)
+    w_relay(3)
+    w_relay(1)
+    cot_out(3)
+    relay(3)
+    w_last(3)
+    handed(2)
+    handed(1)
+    relay(4)
+    ring(3, 1)
+    w_last(1)
+    w_from_core()
+    forward(blocks_of(2))
+    handed(3)
+    forward(blocks_of(1))
+    forward(blocks_of(3))
+    cot_in()
+    backward(blocks_of(2))
+    backward(blocks_of(1))
+    backward(blocks_of(3))
     handed(4)
-    forward([z, ring_block(4, 0)])
-    hidden_out(4)
-    hidden_out(0)
-
+    ring_wait(4, 1)
+    forward(blocks_of(4))
+    backward(blocks_of(4))
     order = [y2, y1, y3, y]
     parts = [(z // 2 + k) % (NZ // 2) for k in (2, 1, 3, 0)]
     core_sum = [[rsem.take() for _ in order] for _ in parts]
@@ -413,12 +489,12 @@
     def lanes_of(pair):
         return pl.ds(mm(pair * 256, 256), 256)
 
-    def gradient(p):
-        for n, yy in enumerate(order):
-            width = ab[:, :, pl.ds(mm(yy * CHUNK + parts[p] * 256, 256), 256)].reshape(TOK, 256)
-            cs[p, n] = dot(dg[1 - c], width).astype(BF).reshape(2, EIGHTH, 256)
-            push(cs.at[p, n], cx.at[p, n], core_sum[p][n], sib)
-            pa[p, n] = dot(dg[c], width).reshape(2, EIGHTH, 256)
+    def gradient(p, n):
+        yy = order[n]
+        width = ab[:, :, pl.ds(mm(yy * CHUNK + parts[p] * 256, 256), 256)].reshape(TOK, 256)
+        cs[p, n] = dot(dg[1 - c], width).astype(BF).reshape(2, EIGHTH, 256)
+        push(cs.at[p, n], cx.at[p, n], core_sum[p][n], sib)
+        pa[p, n] = dot(dg[c], width).reshape(2, EIGHTH, 256)
 
     def send_b(p):
         arrived(cx.at[p, 0], core_sum[p][0])
@@ -458,20 +534,24 @@
             own.start()
             own.wait()
 
-    gradient(0)
-    gradient(1)
+    gradient(0, 0)
+    gradient(1, 0)
+    gradient(2, 0)
     send_b(0)
-    gradient(2)
+    gradient(3, 0)
     send_b(1)
-    send_c(0)
-    gradient(3)
     send_b(2)
-    send_c(1)
+    send_b(3)
+    for k in (4, 3, 5, 2, 6, 1, 7, 0):
+        hidden_out(k)
+    for p in range(4):
+        gradient(p, 1)
+        gradient(p, 2)
+    for p in range(4):
+        send_c(p)
+        gradient(p, 3)
     send_g(0)
-    send_b(3)
-    send_c(2)
     send_g(1)
-    send_c(3)
 
     for k in range(NZ):
         zk = (z + k) % NZ
@@ -481,16 +561,11 @@
             ck = (c + e) % NC
             arrived(hr.at[pl.ds(mm(zk * EIGHTH, 16), EIGHTH), pl.ds(mm(ck * BLK), BLK)],
                     hid_recv + zk * NC + ck)
-    hid[...] = hr[...].astype(F32).T.astype(BF)
-
     send_g(2)
     send_g(3)
     for k in range(1, NZ):
         zk = (z + k) % NZ
         arrived(gr.at[:, pl.ds(mm(zk * EIGHTH, 16), EIGHTH), :], g_recv + zk)
-    both = jnp.concatenate([gr[0], gr[1]], axis=1)
-    wg[...] = dot_nt(interleave_matrix(), both).astype(BF)
-
     def drain(k, _):
         own_copy((t + k) % NT).wait_send()
         return 0
@@ -505,18 +580,19 @@
     any_ = pl.BlockSpec(memory_space=pl.ANY)
     vmem = pl.BlockSpec(memory_space=pltpu.VMEM)
     V = pltpu.VMEM
-    student, hidden, grad = pl.pallas_call(
+    raw = pl.pallas_call(
         kernel,
         out_shape=(
-            jax.ShapeDtypeStruct((256, OWN), BF),
-            jax.ShapeDtypeStruct((256, OWN), BF),
-            jax.ShapeDtypeStruct((256, OWN), BF),
+            jax.ShapeDtypeStruct((OWN, 256), BF),
+            jax.ShapeDtypeStruct((OWN, 256), BF),
+            jax.ShapeDtypeStruct((2, OWN, 128), BF),
         ),
         in_specs=[any_] * 5,
         out_specs=(vmem, vmem, vmem),
         scratch_shapes=[
             V((BLK, D), BF),
             V((256, OWN), BF),
+            V((128, 2, ROWS), BF),
             V((256, ROWS), BF),
             V((1, KEEP), jnp.int32),
             V((1, KEEP), jnp.int32),
@@ -527,13 +603,12 @@
             V((CAP, ROWS), BF),
             V((NT, CAP, 256), BF),
             V((PLACES, 256), BF),
-            V((OWN, 256), BF),
             V((2, OWN, 128), BF),
             V((NC, NY, 2, EIGHTH, CHUNK), BF),
             V((OWN, 256), BF),
             V((NC, EIGHTH, TOK), BF),
             V((NC, EIGHTH, TOK), BF),
-            V((OWN, 256), BF),
+            V((NC, 2, EIGHTH, TOK), F32),
             V((NC, 2 * EIGHTH, TOK), BF),
             V((4, NY, 2, EIGHTH, 256), BF),
             V((4, NY, 2, EIGHTH, 256), BF),
@@ -543,7 +618,6 @@
             V((4, 2, 2, EIGHTH, 256), BF),
             V((4, 2, 2, EIGHTH, 256), BF),
             V((2, EIGHTH, CHUNK), BF),
-            V((2, OWN, 128), BF),
             pltpu.SemaphoreType.DMA((6,)),
             pltpu.SemaphoreType.DMA((224,)),
             pltpu.SemaphoreType.DMA((224,)),
@@ -552,9 +626,25 @@
             collective_id=0, has_side_effects=True, vmem_limit_bytes=60 * 1024 * 1024),
         cost_estimate=pl.CostEstimate(flops=12_000_000_000, bytes_accessed=8_000_000, transcendentals=1_000_000),
         name="student_projection",
-    )(activations, cotangent, old_gate_up.reshape(256, ROWS),
+    )(activations, cotangent, old_gate_up,
       kept_index.reshape(1, KEEP), new_slot.reshape(1, KEEP))
-    return student.reshape(128, 2, OWN), hidden, grad.reshape(128, 2, OWN)
+    return pl.pallas_call(
+        finish,
+        out_shape=(
+            jax.ShapeDtypeStruct((128, 2, OWN), BF),
+            jax.ShapeDtypeStruct((256, OWN), BF),
+            jax.ShapeDtypeStruct((128, 2, OWN), BF),
+        ),
+        in_specs=[any_] * 3,
+        out_specs=(any_,) * 3,
+        scratch_shapes=[
+            V((OWN, 256), BF), V((OWN, 256), BF), V((2, OWN, 128), BF),
+            V((128, 2, OWN), BF), V((256, OWN), BF), V((128, 2, OWN), BF),
+            pltpu.SemaphoreType.DMA((6,)),
+        ],
+        compiler_params=pltpu.CompilerParams(vmem_limit_bytes=60 * 1024 * 1024),
+        name="finish",
+    )(*raw)
 
 
 def solution(mesh):

time: 122 us -> 110 us (0.902); the launches traced: 121 us -> 110 us
  local copies, waits for them, and re-layouts: 9.69 us -> 0 us
    reshape x3 -> x0, local copies, waits for them, and re-layouts: 8.92 us -> none  [the longest x1 4.95 us: per_device(): old_gate_up.reshape(256, ROWS)]
    pallas_call x1 -> x2, Pallas kernels: 110 us -> 109 us  [the longest x1 107 us: per_device(): pl.pallas_call(kernel, out_shape=(jax.ShapeDtypeStruct((OWN, 256), BF), j...]
where the time goes in v3:
time: 110 us
  Pallas kernels  109 us (99%)
    pallas_call x1, Pallas kernels, per_device(): pl.pallas_call(kernel, out_shape=(jax.ShapeDtypeStruct((OWN, 256), BF), j...  107 us
    pallas_call x1, Pallas kernels, per_device(): pl.pallas_call(finish, out_shape=(jax.ShapeDtypeStruct((128, 2, OWN), BF)...  2.63 us

profile of v3, /device:TPU:32, one launch (start us, length us, event | category | flops | bytes accessed | tf_op | source)
XLA Modules:
  0.0 110.1 jit_solution(734075223152459277)
XLA Ops:
  0.6 106.8 %student_projection.1 = (bf16[896,256]{1,0:T(8,128)(2,1)}, bf16[896,256]{1,0:T(8,128)(2,1)}, bf16[2,896,128]{2,1,0:T(8,128)(2,1)}) custom-call(bf16[256,4096]{1,0:T(8,128)(2,1)} %act.1, bf16[256,896]{1,0:T(8,128)(2,1)} %cot.1, bf16[128,2,3584]{2,1,0:T(2,128)(2,1)} %old.1, s32[1,7168]{1,0:T(1,128)} %bitcast.2, s32[1,7168]{1,0:T(1,128)} %bitcast.3), custom_call_target="tpu_custom_call" | custom-call | flops 12000000000 | bytes 8000000 | tf_op jit(solution)/shard_map/student_projection/pallas_call | solution.py:583
  107.4 2.6 %finish.1 = (bf16[128,2,896]{2,1,0:T(2,128)(2,1)}, bf16[256,896]{1,0:T(8,128)(2,1)}, bf16[128,2,896]{2,1,0:T(2,128)(2,1)}) custom-call(bf16[896,256]{1,0:T(8,128)(2,1)} %get-tuple-element.6.stn, bf16[896,256]{1,0:T(8,128)(2,1)} %get-tuple-element.7.hr, bf16[2,896,128]{2,1,0:T(8,128)(2,1)} %get-tuple-element.8.gr), custom_call_target="tpu_custom_call" | custom-call | tf_op jit(solution)/shard_map/finish/pallas_call | solution.py:631

commit v4 on v3

--- a/solution.py
+++ b/solution.py
@@ -307,8 +307,7 @@
     lax.fori_loop(1, NT, own_start, 0)
     rr[pl.ds(mm(t * CAP, 16), CAP), :] = rts[t]
 
-    cot_out(4)
-    cot_push(0, 1)
+    cot_out(2)
     ring(1, 0)
     for k in range(1, NT):
         frm = (t + k) % NT
@@ -435,48 +434,51 @@
                 ck = (c + e) % NC
                 arrived(cb.at[ck, :, pl.ds(mm(zk * BLK), BLK)], cot_recv + zk * NC + ck)
 
+    w_out(1)
     w_out(3)
-    w_out(1)
+    w_out(2)
     ring(2, 0)
-    w_out(2)
     w_round(2)
+    ring(1, 1)
+    w_round(1)
+    relay(1)
     w_round(0)
-    relay(1)
-    ring(1, 1)
+    ring(3, 0)
     w_out(4)
-    ring(3, 0)
+    w_relay(1)
+    w_relay(2)
+    relay(2)
+    cot_out(4)
+    cot_push(0, 1)
     w_relay(0)
+    w_round(3)
     ring(4, 0)
+    cot_out(1)
     ring(2, 1)
-    w_relay(2)
-    cot_out(1)
-    relay(2)
-    cot_out(2)
+    w_relay(3)
     w_last(0)
-    w_round(3)
+    w_last(1)
     w_last(2)
-    w_round(1)
-    w_relay(3)
-    w_relay(1)
+    relay(3)
+    handed(2)
     cot_out(3)
-    relay(3)
+    handed(1)
     w_last(3)
-    handed(2)
-    handed(1)
+    w_from_core()
+    ring(3, 1)
     relay(4)
-    ring(3, 1)
-    w_last(1)
-    w_from_core()
+    forward(blocks_of(1))
     forward(blocks_of(2))
     handed(3)
-    forward(blocks_of(1))
     forward(blocks_of(3))
+    for k in (3, 5, 2, 6, 1, 7):
+        hidden_out(k)
     cot_in()
+    backward(blocks_of(1))
     backward(blocks_of(2))
-    backward(blocks_of(1))
     backward(blocks_of(3))
+    ring_wait(4, 1)
     handed(4)
-    ring_wait(4, 1)
     forward(blocks_of(4))
     backward(blocks_of(4))
     order = [y2, y1, y3, y]
@@ -535,23 +537,35 @@
             own.wait()
 
     gradient(0, 0)
+    gradient(2, 2)
     gradient(1, 0)
     gradient(2, 0)
+    gradient(0, 1)
     send_b(0)
+    gradient(0, 2)
+    send_b(1)
+    gradient(1, 2)
+    hidden_out(4)
+    send_b(2)
+    gradient(1, 1)
+    send_c(0)
+    gradient(0, 3)
     gradient(3, 0)
-    send_b(1)
-    send_b(2)
+    gradient(2, 1)
+    send_c(1)
+    gradient(3, 1)
+    gradient(3, 2)
     send_b(3)
-    for k in (4, 3, 5, 2, 6, 1, 7, 0):
-        hidden_out(k)
-    for p in range(4):
-        gradient(p, 1)
-        gradient(p, 2)
-    for p in range(4):
-        send_c(p)
-        gradient(p, 3)
     send_g(0)
+    send_c(2)
+    gradient(1, 3)
+    hidden_out(0)
+    gradient(2, 3)
+    send_c(3)
     send_g(1)
+    gradient(3, 3)
+    send_g(2)
+    send_g(3)
 
     for k in range(NZ):
         zk = (z + k) % NZ
@@ -561,8 +575,6 @@
             ck = (c + e) % NC
             arrived(hr.at[pl.ds(mm(zk * EIGHTH, 16), EIGHTH), pl.ds(mm(ck * BLK), BLK)],
                     hid_recv + zk * NC + ck)
-    send_g(2)
-    send_g(3)
     for k in range(1, NZ):
         zk = (z + k) % NZ
         arrived(gr.at[:, pl.ds(mm(zk * EIGHTH, 16), EIGHTH), :], g_recv + zk)

time: 110 us -> 107 us (0.973)
  Pallas kernels: 109 us -> 106 us
    pallas_call x1, Pallas kernels: 107 us -> 103 us  [per_device(): pl.pallas_call(kernel, out_shape=(jax.ShapeDtypeStruct((OWN, 256), BF), j...]
where the time goes in v4:
time: 107 us
  Pallas kernels  106 us (99%)
    pallas_call x1, Pallas kernels, per_device(): pl.pallas_call(kernel, out_shape=(jax.ShapeDtypeStruct((OWN, 256), BF), j...  103 us
    pallas_call x1, Pallas kernels, per_device(): pl.pallas_call(finish, out_shape=(jax.ShapeDtypeStruct((128, 2, OWN), BF)...  2.63 us

profile of v4, /device:TPU:32, one launch (start us, length us, event | category | flops | bytes accessed | tf_op | source)
XLA Modules:
  0.0 106.8 jit_solution(2241044306364306173)
XLA Ops:
  0.6 103.5 %student_projection.1 = (bf16[896,256]{1,0:T(8,128)(2,1)}, bf16[896,256]{1,0:T(8,128)(2,1)}, bf16[2,896,128]{2,1,0:T(8,128)(2,1)}) custom-call(bf16[256,4096]{1,0:T(8,128)(2,1)} %act.1, bf16[256,896]{1,0:T(8,128)(2,1)} %cot.1, bf16[128,2,3584]{2,1,0:T(2,128)(2,1)} %old.1, s32[1,7168]{1,0:T(1,128)} %bitcast.2, s32[1,7168]{1,0:T(1,128)} %bitcast.3), custom_call_target="tpu_custom_call" | custom-call | flops 12000000000 | bytes 8000000 | tf_op jit(solution)/shard_map/student_projection/pallas_call | solution.py:595
  104.1 2.6 %finish.1 = (bf16[128,2,896]{2,1,0:T(2,128)(2,1)}, bf16[256,896]{1,0:T(8,128)(2,1)}, bf16[128,2,896]{2,1,0:T(2,128)(2,1)}) custom-call(bf16[896,256]{1,0:T(8,128)(2,1)} %get-tuple-element.6.stn, bf16[896,256]{1,0:T(8,128)(2,1)} %get-tuple-element.7.hr, bf16[2,896,128]{2,1,0:T(8,128)(2,1)} %get-tuple-element.8.gr), custom_call_target="tpu_custom_call" | custom-call | tf_op jit(solution)/shard_map/finish/pallas_call | solution.py:643

commit v5 on v4

--- a/solution.py
+++ b/solution.py
@@ -291,14 +291,13 @@
             device_id=(dp, to), device_id_type=MESH)
 
     def select(k, _):
-        to = (t + k) % NT
-        row = iota((CAP, 128), 0) + (to * CAP + 1)
+        row = iota((2 * CAP, 128), 0) + (k * (2 * CAP) + 1)
         for h in range(ROWS // 128):
             pb[:, h * 128:(h + 1) * 128] = onehot(place_s[h:h + 1, :] == row)
-        rts[to] = dot_nt(pb[...], o_two[...]).astype(BF)
+        rts[pl.ds(2 * k, 2)] = dot_nt(pb[...], o_two[...]).astype(BF).reshape(2, CAP, 256)
         return 0
 
-    lax.fori_loop(0, NT, select, 0)
+    lax.fori_loop(0, NT // 2, select, 0)
 
     def own_start(k, _):
         own_copy((t + k) % NT).start()
@@ -612,7 +611,7 @@
             V((8, KEEP), jnp.int32),
             V((KB * 16, 128), BF),
             V((KB * 16, 128), F32),
-            V((CAP, ROWS), BF),
+            V((2 * CAP, ROWS), BF),
             V((NT, CAP, 256), BF),
             V((PLACES, 256), BF),
             V((2, OWN, 128), BF),

time: 107 us -> 104 us (0.972)
  Pallas kernels: 106 us -> 104 us
    pallas_call x1, Pallas kernels: 103 us -> 101 us  [per_device(): pl.pallas_call(kernel, out_shape=(jax.ShapeDtypeStruct((OWN, 256), BF), j...]
where the time goes in v5:
time: 104 us
  Pallas kernels  104 us (100%)
    pallas_call x1, Pallas kernels, per_device(): pl.pallas_call(kernel, out_shape=(jax.ShapeDtypeStruct((OWN, 256), BF), j...  101 us
    pallas_call x1, Pallas kernels, per_device(): pl.pallas_call(finish, out_shape=(jax.ShapeDtypeStruct((128, 2, OWN), BF)...  2.63 us

profile of v5, /device:TPU:32, one launch (start us, length us, event | category | flops | bytes accessed | tf_op | source)
XLA Modules:
  0.0 104.3 jit_solution(12751956110073179227)
XLA Ops:
  0.6 101.0 %student_projection.1 = (bf16[896,256]{1,0:T(8,128)(2,1)}, bf16[896,256]{1,0:T(8,128)(2,1)}, bf16[2,896,128]{2,1,0:T(8,128)(2,1)}) custom-call(bf16[256,4096]{1,0:T(8,128)(2,1)} %act.1, bf16[256,896]{1,0:T(8,128)(2,1)} %cot.1, bf16[128,2,3584]{2,1,0:T(2,128)(2,1)} %old.1, s32[1,7168]{1,0:T(1,128)} %bitcast.2, s32[1,7168]{1,0:T(1,128)} %bitcast.3), custom_call_target="tpu_custom_call" | custom-call | flops 12000000000 | bytes 8000000 | tf_op jit(solution)/shard_map/student_projection/pallas_call | solution.py:594
  101.6 2.6 %finish.1 = (bf16[128,2,896]{2,1,0:T(2,128)(2,1)}, bf16[256,896]{1,0:T(8,128)(2,1)}, bf16[128,2,896]{2,1,0:T(2,128)(2,1)}) custom-call(bf16[896,256]{1,0:T(8,128)(2,1)} %get-tuple-element.6.stn, bf16[896,256]{1,0:T(8,128)(2,1)} %get-tuple-element.7.hr, bf16[2,896,128]{2,1,0:T(8,128)(2,1)} %get-tuple-element.8.gr), custom_call_target="tpu_custom_call" | custom-call | tf_op jit(solution)/shard_map/finish/pallas_call | solution.py:642
